TPU v7x, 32 devices: a whole 2x2x4 slice. The times are simulated.
32 devices in a mesh: inline: 8 (over z, x), xline: 4 (over y, core).
Axes of the slice: x: 2, y: 2, z: 4, core: 2. Of those that a mesh axis runs over, the one named last changes fastest.
Arguments:
- traces: bfloat16 [8192, 2048], P(('inline', 'xline')), may hold values from -6 to 6
- trace_dest: int32 [8192, 1], P(('inline', 'xline')), may hold values from 0 to 31; in each aligned block of 256 rows (0 to 255, 256 to 511, ...) at most 16 rows name the same one
- trace_bin: int32 [8192], P(('inline', 'xline')), may hold values from 0 to 3
- trace_class: int32 [8192], P(('inline', 'xline')), may hold values from 0 to 7
- band_weights: bfloat16 [8, 16, 2, 128, 128], replicated, may hold values from -0.375 to 0.375
- conv_first: bfloat16 [32, 8, 3, 3, 3], replicated, may hold values from -0.4375 to 0.4375
- conv_second: bfloat16 [32, 32, 3, 3, 3], replicated, may hold values from -0.21875 to 0.21875
Outputs:
- regular: bfloat16 [32, 16, 8, 2048], P(None, 'inline', 'xline')
Inputs may be any that keep to these rules, and one draw needn't show every extreme that they name: `trace_dest`: among the 256 traces of one device no tile is named more than 16 times, a bound that some block reaches.
All inputs are finite; a program needn't handle non-finite values.
Results may differ from a plain program's by a relative error of at most 0.0065.
Values may be sent and summed in bfloat16 or wider, within the bound.
A program may use at most 256 MiB of HBM per device.

v0:
```python
import jax
import jax.numpy as jnp
from jax import lax
from jax.sharding import PartitionSpec as P

CLASSES = 8
BI = 2
BX = 2


def padded_2(block, sides, width):
    for axis, dim in sides:
        count = lax.axis_size(axis)
        forward = [(i, i + 1) for i in range(count - 1)]
        backward = [(target, source) for source, target in forward]
        low = lax.ppermute(
            lax.slice_in_dim(block, block.shape[dim] - width, None, axis=dim), axis, forward
        )
        high = lax.ppermute(lax.slice_in_dim(block, 0, width, axis=dim), axis, backward)
        block = jnp.concatenate([low, block, high], axis=dim)
    return block


def convolve(padded, kernel):
    inner_i = padded.shape[1] - 2
    inner_x = padded.shape[2] - 2
    samples = padded.shape[3]
    timed = jnp.pad(padded, ((0, 0), (0, 0), (0, 0), (1, 1)))
    total = jnp.zeros((kernel.shape[0], inner_i, inner_x, samples), jnp.float32)
    for first in range(3):
        for second in range(3):
            for third in range(3):
                window = timed[
                    :, first : first + inner_i, second : second + inner_x, third : third + samples
                ]
                total = total + jnp.einsum(
                    "oc,cijs->oijs",
                    kernel[:, :, first, second, third],
                    window,
                    preferred_element_type=jnp.float32,
                )
    return total


def per_device(traces, trace_dest, trace_bin, trace_class, band_weights, conv_first, conv_second):
    inline_size = lax.axis_size("inline")
    xline_size = lax.axis_size("xline")
    devices_all = inline_size * xline_size
    trace_total, samples = traces.shape
    capacity = max(2, 2 * trace_total // devices_all)
    band_width = band_weights.shape[-1]
    target = trace_dest[:, 0]
    order = jnp.arange(trace_total, dtype=jnp.int32)
    earlier = (target[:, None] == target[None, :]) & (order[None, :] < order[:, None])
    slot_index = jnp.sum(earlier.astype(jnp.int32), axis=1)
    position = target * capacity + slot_index
    tile_bins = BI * BX
    bin_code = trace_class * tile_bins + trace_bin
    outgoing = jnp.zeros((devices_all * capacity, samples), jnp.bfloat16).at[position].set(traces)
    out_codes = jnp.full((devices_all * capacity,), -1, jnp.int32).at[position].set(bin_code)
    arrived, arrived_codes = (
        lax.all_to_all(
            outgoing.reshape(devices_all, capacity, samples),
            ("inline", "xline"),
            split_axis=0,
            concat_axis=0,
            tiled=True,
        ),
        lax.all_to_all(
            out_codes.reshape(devices_all, capacity),
            ("inline", "xline"),
            split_axis=0,
            concat_axis=0,
            tiled=True,
        ),
    )
    arrived = arrived.reshape(devices_all * capacity, samples)
    arrived_codes = arrived_codes.reshape(devices_all * capacity)
    cells = jnp.arange(CLASSES * tile_bins, dtype=jnp.int32)
    selector = (cells[:, None] == arrived_codes[None, :]).astype(jnp.bfloat16)
    stacked = jnp.dot(selector, arrived, preferred_element_type=jnp.float32)
    fold_count = jnp.sum(selector.astype(jnp.float32), axis=1)
    averaged = (stacked / jnp.maximum(fold_count, 1.0)[:, None]).astype(jnp.bfloat16)
    blocks = averaged.reshape(CLASSES, tile_bins, samples // band_width, band_width)
    following = jnp.concatenate([blocks[:, :, 1:], jnp.zeros_like(blocks[:, :, :1])], axis=2)
    shifted = jnp.einsum(
        "cbkt,cktu->cbku", blocks, band_weights[:, :, 0], preferred_element_type=jnp.float32
    )
    shifted = shifted + jnp.einsum(
        "cbkt,cktu->cbku", following, band_weights[:, :, 1], preferred_element_type=jnp.float32
    )
    volume = shifted.astype(jnp.bfloat16).reshape(CLASSES, BI, BX, samples)
    padded = padded_2(volume, (("inline", 1), ("xline", 2)), 1)
    hidden = jax.nn.gelu(convolve(padded, conv_first)).astype(jnp.bfloat16)
    hidden_padded = padded_2(hidden, (("inline", 1), ("xline", 2)), 1)
    return convolve(hidden_padded, conv_second).astype(jnp.bfloat16)


def solution(mesh):
    return jax.shard_map(
        per_device,
        mesh=mesh,
        in_specs=(
            P(("inline", "xline"), None),
            P(("inline", "xline"), None),
            P(("inline", "xline")),
            P(("inline", "xline")),
            P(),
            P(),
            P(),
        ),
        out_specs=P(None, "inline", "xline", None),
        check_vma=False,
    )
```

profile of v0, /device:TPU:1, one launch (start us, length us, event | category | flops | bytes accessed | tf_op | source)
XLA Modules:
  0.0 144.3 jit_solution(13763838275985503138)
XLA Ops:
  0.0 0.9 convert_reduce_fusion
  0.9 0.7 compare_select_fusion
  1.6 0.7 multiply_add_fusion
  2.3 1.4 scatter_custom_fusion
  3.7 0.7 all_to_all.9
  4.4 7.1 %all-to-all-start = ((s32[32,1,16]{2,1,0:T(1,128)}), s32[32,1,16]{2,1,0:T(1,128)S(1)}, u32[]{:S(2)}, u32[]{:S(2)}) async-start(s32[32,1,16]{2,1,0:T(1,128)} %bitcast.3), calls=%async_computation | async-start | bytes 32768 | tf_op jit(solution)/shard_map/all_to_all | solution.py:69
  11.5 4.4 %scatter_custom_fusion.1 = bf16[512,2048]{1,0:T(8,128)(2,1)} fusion(s32[256]{0:T(256)S(1)} %bitcast.509, bf16[256,2048]{1,0:T(8,128)(2,1)} %param.7, bf16[]{:T(256)} %constant.3.clone.1), kind=kCustom, calls=%fused_computation.114 | custom fusion | bytes 2097664 | tf_op jit(solution)/shard_map/scatter | solution.py:59
  15.9 2.3 %all-to-all-done = s32[32,1,16]{2,1,0:T(1,128)S(1)} async-done(((s32[32,1,16]{2,1,0:T(1,128)}), s32[32,1,16]{2,1,0:T(1,128)S(1)}, u32[]{:S(2)}, u32[]{:S(2)}) %all-to-all-start) | async-done | bytes 2080 | tf_op jit(solution)/shard_map/all_to_all | solution.py:69
  18.2 3.6 %all-to-all-start.1 = ((bf16[32,16,2048]{2,1,0:T(8,128)(2,1)}), bf16[32,16,2048]{2,1,0:T(8,128)(2,1)S(1)}, u32[]{:S(2)}, u32[]{:S(2)}) async-start(bf16[32,16,2048]{2,1,0:T(8,128)(2,1)} %bitcast.4), calls=%async_computation.1 | async-start | bytes 4194304 | tf_op jit(solution)/shard_map/all_to_all | solution.py:62
  21.8 0.5 broadcast.92
  22.3 0.7 reduce.3
  23.2 46.7 %all-to-all-done.1 = bf16[32,16,2048]{2,1,0:T(8,128)(2,1)S(1)} async-done(((bf16[32,16,2048]{2,1,0:T(8,128)(2,1)}), bf16[32,16,2048]{2,1,0:T(8,128)(2,1)S(1)}, u32[]{:S(2)}, u32[]{:S(2)}) %all-to-all-start.1) | async-done | bytes 2097184 | tf_op jit(solution)/shard_map/all_to_all | solution.py:62
  70.0 0.5 fusion.57
  70.5 3.4 %fusion.1 = f32[8,16,4,128]{3,2,1,0:T(4,128)S(1)} fusion(bf16[8,16,2,128,128]{4,3,2,1,0:T(8,128)(2,1)} %param.11, bf16[8,4,16,128]{3,1,2,0:T(4,128)(2,1)S(1)} %copy.28), kind=kOutput, calls=%fused_computation.5 | convolution fusion | flops 15728640 | bytes 4579328 | tf_op jit(solution)/shard_map/cbkt,cktu->cbku/dot_general | solution.py:89
  73.9 3.4 %fusion.54 = bf16[8,4,16,128]{3,1,2,0:T(4,128)(2,1)S(1)} fusion(f32[8,16,4,128]{3,2,1,0:T(4,128)S(1)} %fusion.1, bf16[8,16,2,128,128]{4,3,2,1,0:T(8,128)(2,1)} %param.11, bf16[8,4,16,128]{3,2,1,0:T(8,128)(2,1)S(1)} %bitcast.505), kind=kOutput, calls=%fused_computation.102 | convolution fusion | flops 16908288 | bytes 4718592 | tf_op jit(solution)/shard_map/cbkt,cktu->cbku/dot_general | solution.py:86
  77.4 3.0 %collective-permute-start = (bf16[8,1,2,2048]{3,0,2,1:T(8,128)(2,1)S(1)}, bf16[8,1,2,2048]{3,0,2,1:T(8,128)(2,1)S(1)}, u32[]{:S(2)}, u32[]{:S(2)}) collective-permute-start(bf16[8,1,2,2048]{3,0,2,1:T(8,128)(2,1)S(1)} %get-tuple-element.14), channel_id=1, source_target_pairs={{0,4},{4,8},{8,12},{12,16},{16,20},{20,24},{24,28},{1,5},{5,9},{9,... | collective-permute-start | bytes 196616 | tf_op jit(solution)/shard_map/ppermute | solution.py:16
  80.5 1.3 collective-permute-start.1
  81.8 3.7 %collective-permute-done.1 = bf16[8,1,2,2048]{3,0,2,1:T(8,128)(2,1)S(1)} collective-permute-done((bf16[8,1,2,2048]{3,0,2,1:T(8,128)(2,1)S(1)}, bf16[8,1,2,2048]{3,0,2,1:T(8,128)(2,1)S(1)}, u32[]{:S(2)}, u32[]{:S(2)}) %collective-permute-start.1) | collective-permute-done | bytes 65568 | tf_op jit(solution)/shard_map/ppermute | solution.py:19
  85.5 5.3 %collective-permute-start.2 = (bf16[8,4,1,2048]{3,0,2,1:T(8,128)(2,1)S(1)}, bf16[8,4,1,2048]{3,0,2,1:T(8,128)(2,1)S(1)}, u32[]{:S(2)}, u32[]{:S(2)}) collective-permute-start(bf16[8,4,1,2048]{3,0,2,1:T(8,128)(2,1)S(1)} %get-tuple-element.11), channel_id=1, source_target_pairs={{0,1},{1,2},{2,3},{4,5},{5,6},{6,7},{8,9},{9,10},{10,11},{12,13},{... | collective-permute-start | bytes 393224 | tf_op jit(solution)/shard_map/ppermute | solution.py:16
  90.9 2.1 %collective-permute-start.3 = (bf16[8,4,1,2048]{3,0,2,1:T(8,128)(2,1)S(1)}, bf16[8,4,1,2048]{3,0,2,1:T(8,128)(2,1)S(1)}, u32[]{:S(2)}, u32[]{:S(2)}) collective-permute-start(bf16[8,4,1,2048]{3,0,2,1:T(8,128)(2,1)S(1)} %get-tuple-element.12), channel_id=1, source_target_pairs={{1,0},{2,1},{3,2},{5,4},{6,5},{7,6},{9,8},{10,9},{11,10},{13,12},{... | collective-permute-start | bytes 393224 | tf_op jit(solution)/shard_map/ppermute | solution.py:19
  93.3 3.8 %collective-permute-done.3 = bf16[8,4,1,2048]{3,0,2,1:T(8,128)(2,1)S(1)} collective-permute-done((bf16[8,4,1,2048]{3,0,2,1:T(8,128)(2,1)S(1)}, bf16[8,4,1,2048]{3,0,2,1:T(8,128)(2,1)S(1)}, u32[]{:S(2)}, u32[]{:S(2)}) %collective-permute-start.3) | collective-permute-done | bytes 131104 | tf_op jit(solution)/shard_map/ppermute | solution.py:19
  104.9 0.9 fusion.22
  107.1 0.6 fusion.66
  107.8 2.6 %collective-permute-start.4 = (bf16[32,1,2,2048]{3,0,2,1:T(8,128)(2,1)S(1)}, bf16[32,1,2,2048]{3,0,2,1:T(8,128)(2,1)S(1)}, u32[]{:S(2)}, u32[]{:S(2)}) collective-permute-start(bf16[32,1,2,2048]{3,0,2,1:T(8,128)(2,1)S(1)} %get-tuple-element.9), channel_id=1, source_target_pairs={{0,4},{4,8},{8,12},{12,16},{16,20},{20,24},{24,28},{1,5},{5,9},{9,... | collective-permute-start | bytes 786440 | tf_op jit(solution)/shard_map/ppermute | solution.py:16
  110.3 1.3 collective-permute-start.5
  111.6 7.8 %collective-permute-done.4 = bf16[32,1,2,2048]{3,0,2,1:T(8,128)(2,1)S(1)} collective-permute-done((bf16[32,1,2,2048]{3,0,2,1:T(8,128)(2,1)S(1)}, bf16[32,1,2,2048]{3,0,2,1:T(8,128)(2,1)S(1)}, u32[]{:S(2)}, u32[]{:S(2)}) %collective-permute-start.4) | collective-permute-done | bytes 262176 | tf_op jit(solution)/shard_map/ppermute | solution.py:16
  119.7 2.1 %collective-permute-start.6 = (bf16[32,4,1,2048]{3,0,2,1:T(8,128)(2,1)S(1)}, bf16[32,4,1,2048]{3,0,2,1:T(8,128)(2,1)S(1)}, u32[]{:S(2)}, u32[]{:S(2)}) collective-permute-start(bf16[32,4,1,2048]{3,0,2,1:T(8,128)(2,1)S(1)} %get-tuple-element.7), channel_id=1, source_target_pairs={{0,1},{1,2},{2,3},{4,5},{5,6},{6,7},{8,9},{9,10},{10,11},{12,13},{... | collective-permute-start | bytes 1572872 | tf_op jit(solution)/shard_map/ppermute | solution.py:16
  121.7 2.7 %collective-permute-start.7 = (bf16[32,4,1,2048]{3,0,2,1:T(8,128)(2,1)S(1)}, bf16[32,4,1,2048]{3,0,2,1:T(8,128)(2,1)S(1)}, u32[]{:S(2)}, u32[]{:S(2)}) collective-permute-start(bf16[32,4,1,2048]{3,0,2,1:T(8,128)(2,1)S(1)} %get-tuple-element.8), channel_id=1, source_target_pairs={{1,0},{2,1},{3,2},{5,4},{6,5},{7,6},{9,8},{10,9},{11,10},{13,12},{... | collective-permute-start | bytes 1572872 | tf_op jit(solution)/shard_map/ppermute | solution.py:19
  124.4 3.4 %collective-permute-done.6 = bf16[32,4,1,2048]{3,0,2,1:T(8,128)(2,1)S(1)} collective-permute-done((bf16[32,4,1,2048]{3,0,2,1:T(8,128)(2,1)S(1)}, bf16[32,4,1,2048]{3,0,2,1:T(8,128)(2,1)S(1)}, u32[]{:S(2)}, u32[]{:S(2)}) %collective-permute-start.6) | collective-permute-done | bytes 524320 | tf_op jit(solution)/shard_map/ppermute | solution.py:16
  127.9 4.4 %collective-permute-done.7 = bf16[32,4,1,2048]{3,0,2,1:T(8,128)(2,1)S(1)} collective-permute-done((bf16[32,4,1,2048]{3,0,2,1:T(8,128)(2,1)S(1)}, bf16[32,4,1,2048]{3,0,2,1:T(8,128)(2,1)S(1)}, u32[]{:S(2)}, u32[]{:S(2)}) %collective-permute-start.7) | collective-permute-done | bytes 524320 | tf_op jit(solution)/shard_map/ppermute | solution.py:19
  132.2 1.8 %select_maximum_fusion = bf16[32,4,4,2050]{3,0,2,1:T(8,128)(2,1)S(1)} fusion(bf16[32,4,1,2048]{3,0,2,1:T(8,128)(2,1)S(1)} %collective-permute-done.7, bf16[32,4,1,2048]{3,0,2,1:T(8,128)(2,1)S(1)} %collective-permute-done.6, bf16[32,1,2,2048]{3,0,2,1:T(8,128)(2,1)S(1)} %collective-permute-done.5, bf16[32,2,2,2048]{3,0,2,1:T(8,128)(2,1)S(1)} %fusion.66, ...), kind=kLoop, calls=%fused_computation.88 | loop fusion | flops 18892800 | bytes 4196352 | tf_op jit(solution)/shard_map/concatenate | solution.py:20
  142.9 1.3 copy.32
  (76 shorter events, 18.6 us)
Async XLA Ops:
  4.4 13.8 %all-to-all-start = ((s32[32,1,16]{2,1,0:T(1,128)}), s32[32,1,16]{2,1,0:T(1,128)S(1)}, u32[]{:S(2)}, u32[]{:S(2)}) async-start(s32[32,1,16]{2,1,0:T(1,128)} %bitcast.3), calls=%async_computation | async-start | bytes 32768 | tf_op jit(solution)/shard_map/all_to_all | solution.py:69
  18.2 51.7 %all-to-all-start.1 = ((bf16[32,16,2048]{2,1,0:T(8,128)(2,1)}), bf16[32,16,2048]{2,1,0:T(8,128)(2,1)S(1)}, u32[]{:S(2)}, u32[]{:S(2)}) async-start(bf16[32,16,2048]{2,1,0:T(8,128)(2,1)} %bitcast.4), calls=%async_computation.1 | async-start | bytes 4194304 | tf_op jit(solution)/shard_map/all_to_all | solution.py:62
  73.9 19.1 %copy-start.1 = (bf16[32,8,3,3,3]{0,1,4,3,2:T(8,128)(2,1)S(1)}, bf16[32,8,3,3,3]{0,1,4,3,2:T(8,128)(2,1)}, u32[]{:S(2)}) copy-start(bf16[32,8,3,3,3]{0,1,4,3,2:T(8,128)(2,1)} %param.12) | copy-start | bytes 41476
  77.4 4.3 %collective-permute-start = (bf16[8,1,2,2048]{3,0,2,1:T(8,128)(2,1)S(1)}, bf16[8,1,2,2048]{3,0,2,1:T(8,128)(2,1)S(1)}, u32[]{:S(2)}, u32[]{:S(2)}) collective-permute-start(bf16[8,1,2,2048]{3,0,2,1:T(8,128)(2,1)S(1)} %get-tuple-element.14), channel_id=1, source_target_pairs={{0,4},{4,8},{8,12},{12,16},{16,20},{20,24},{24,28},{1,5},{5,9},{9,... | collective-permute-start | bytes 196616 | tf_op jit(solution)/shard_map/ppermute | solution.py:16
  80.5 5.0 %collective-permute-start.1 = (bf16[8,1,2,2048]{3,0,2,1:T(8,128)(2,1)S(1)}, bf16[8,1,2,2048]{3,0,2,1:T(8,128)(2,1)S(1)}, u32[]{:S(2)}, u32[]{:S(2)}) collective-permute-start(bf16[8,1,2,2048]{3,0,2,1:T(8,128)(2,1)S(1)} %get-tuple-element.13), channel_id=1, source_target_pairs={{4,0},{8,4},{12,8},{16,12},{20,16},{24,20},{28,24},{5,1},{9,5},{13... | collective-permute-start | bytes 196616 | tf_op jit(solution)/shard_map/ppermute | solution.py:19
  85.5 7.8 %collective-permute-start.2 = (bf16[8,4,1,2048]{3,0,2,1:T(8,128)(2,1)S(1)}, bf16[8,4,1,2048]{3,0,2,1:T(8,128)(2,1)S(1)}, u32[]{:S(2)}, u32[]{:S(2)}) collective-permute-start(bf16[8,4,1,2048]{3,0,2,1:T(8,128)(2,1)S(1)} %get-tuple-element.11), channel_id=1, source_target_pairs={{0,1},{1,2},{2,3},{4,5},{5,6},{6,7},{8,9},{9,10},{10,11},{12,13},{... | collective-permute-start | bytes 393224 | tf_op jit(solution)/shard_map/ppermute | solution.py:16
  90.9 6.3 %collective-permute-start.3 = (bf16[8,4,1,2048]{3,0,2,1:T(8,128)(2,1)S(1)}, bf16[8,4,1,2048]{3,0,2,1:T(8,128)(2,1)S(1)}, u32[]{:S(2)}, u32[]{:S(2)}) collective-permute-start(bf16[8,4,1,2048]{3,0,2,1:T(8,128)(2,1)S(1)} %get-tuple-element.12), channel_id=1, source_target_pairs={{1,0},{2,1},{3,2},{5,4},{6,5},{7,6},{9,8},{10,9},{11,10},{13,12},{... | collective-permute-start | bytes 393224 | tf_op jit(solution)/shard_map/ppermute | solution.py:19
  107.8 11.7 %collective-permute-start.4 = (bf16[32,1,2,2048]{3,0,2,1:T(8,128)(2,1)S(1)}, bf16[32,1,2,2048]{3,0,2,1:T(8,128)(2,1)S(1)}, u32[]{:S(2)}, u32[]{:S(2)}) collective-permute-start(bf16[32,1,2,2048]{3,0,2,1:T(8,128)(2,1)S(1)} %get-tuple-element.9), channel_id=1, source_target_pairs={{0,4},{4,8},{8,12},{12,16},{16,20},{20,24},{24,28},{1,5},{5,9},{9,... | collective-permute-start | bytes 786440 | tf_op jit(solution)/shard_map/ppermute | solution.py:16
  110.3 9.1 %collective-permute-start.5 = (bf16[32,1,2,2048]{3,0,2,1:T(8,128)(2,1)S(1)}, bf16[32,1,2,2048]{3,0,2,1:T(8,128)(2,1)S(1)}, u32[]{:S(2)}, u32[]{:S(2)}) collective-permute-start(bf16[32,1,2,2048]{3,0,2,1:T(8,128)(2,1)S(1)} %get-tuple-element.10), channel_id=1, source_target_pairs={{4,0},{8,4},{12,8},{16,12},{20,16},{24,20},{28,24},{5,1},{9,5},{13... | collective-permute-start | bytes 786440 | tf_op jit(solution)/shard_map/ppermute | solution.py:19
  119.7 14.3 %copy-start = (bf16[32,32,3,3,3]{1,0,4,3,2:T(8,128)(2,1)S(1)}, bf16[32,32,3,3,3]{1,0,4,3,2:T(8,128)(2,1)}, u32[]{:S(2)}) copy-start(bf16[32,32,3,3,3]{1,0,4,3,2:T(8,128)(2,1)} %param.13) | copy-start | bytes 165892
  119.7 8.2 %collective-permute-start.6 = (bf16[32,4,1,2048]{3,0,2,1:T(8,128)(2,1)S(1)}, bf16[32,4,1,2048]{3,0,2,1:T(8,128)(2,1)S(1)}, u32[]{:S(2)}, u32[]{:S(2)}) collective-permute-start(bf16[32,4,1,2048]{3,0,2,1:T(8,128)(2,1)S(1)} %get-tuple-element.7), channel_id=1, source_target_pairs={{0,1},{1,2},{2,3},{4,5},{5,6},{6,7},{8,9},{9,10},{10,11},{12,13},{... | collective-permute-start | bytes 1572872 | tf_op jit(solution)/shard_map/ppermute | solution.py:16
  121.7 10.5 %collective-permute-start.7 = (bf16[32,4,1,2048]{3,0,2,1:T(8,128)(2,1)S(1)}, bf16[32,4,1,2048]{3,0,2,1:T(8,128)(2,1)S(1)}, u32[]{:S(2)}, u32[]{:S(2)}) collective-permute-start(bf16[32,4,1,2048]{3,0,2,1:T(8,128)(2,1)S(1)} %get-tuple-element.8), channel_id=1, source_target_pairs={{1,0},{2,1},{3,2},{5,4},{6,5},{7,6},{9,8},{10,9},{11,10},{13,12},{... | collective-permute-start | bytes 1572872 | tf_op jit(solution)/shard_map/ppermute | solution.py:19
where the time goes:
time: 145 us; the launch traced here: 144 us
  waiting for transfers between devices  72.2 us (50%)
  starting transfers between devices  31 us (21%)
  matrix products  26 us (18%)
  local copies, waits for them, and re-layouts  8.78 us (6%)
  other arithmetic  5.65 us (4%)
    all_to_all x1, waiting for transfers between devices, per_device(): lax.all_to_all(outgoing.reshape(devices_all, capacity, samples), ('inline...  46.7 us
    dot_general x54, matrix products, convolve(): jnp.einsum('oc,cijs->oijs', kernel[:, :, first, second, third], window, p...  18.8 us
    ppermute x4, starting transfers between devices, padded_2(): lax.ppermute(lax.slice_in_dim(block, block.shape[dim] - width, None, axis...  13 us
    ppermute x4, waiting for transfers between devices, padded_2(): lax.ppermute(lax.slice_in_dim(block, 0, width, axis=dim), axis, backward)  11.9 us
    ppermute x4, waiting for transfers between devices, padded_2(): lax.ppermute(lax.slice_in_dim(block, block.shape[dim] - width, None, axis...  11.3 us
    ppermute x4, starting transfers between devices, padded_2(): lax.ppermute(lax.slice_in_dim(block, 0, width, axis=dim), axis, backward)  7.34 us
    all_to_all x1, starting transfers between devices, per_device(): lax.all_to_all(out_codes.reshape(devices_all, capacity), ('inline', 'xlin...  7.1 us
    scatter x1, local copies, waits for them, and re-layouts, per_device(): jnp.zeros((devices_all * capacity, samples), jnp.bfloat16).at[position]  4.43 us
  transfers between devices with their start and end apart: 10, of which 7 were waited for; matrix products, arithmetic and copies ran while one was open for 4% of the time, Pallas kernels for 0%

commit v1 on v0

v1 whole, which is shorter than its diff:
```python
import functools

import jax
import jax.numpy as jnp
from jax import lax
from jax.experimental import pallas as pl
from jax.experimental.pallas import tpu as pltpu
from jax.sharding import PartitionSpec as P

CLASSES = 8
BI = 2
BX = 2
GI = 2
LANES = 128
MESH = pl.DeviceIdType.MESH
F32 = jnp.float32
BF16 = jnp.bfloat16


def gelu(x):
    return 0.5 * x * (1.0 + jnp.tanh(0.7978845608028654 * (x + 0.044715 * (x * x * x))))


def kernel(
    planes, xsize, rows, samples, ch,
    traces, codes, band, k1, k2, out,
    rx, crx, oh, own, cown, txz, rz, ctx, crz, avg, anx, wts, vol, nxt, prv, v3, h3, t1, t2, outb,
    w_sem, l_sem, o_sem, a_send, a_recv, c_send, c_recv, z_send, z_recv, n_send, n_recv,
    e_send, e_recv, g_send, g_recv, y_send, y_recv,
):
    T = GI * xsize
    R = planes
    S = samples // T
    NCH = S // LANES
    I = GI * BI
    XL = xsize * BX
    CELLS = CLASSES * I * XL
    VR = CLASSES * XL
    HR = ch * XL
    inline = lax.axis_index("inline")
    xline = lax.axis_index("xline")
    z = lax.div(inline, GI)
    t = lax.rem(inline, GI) * xsize + xline

    def dev(zz, tt):
        return (zz * GI + lax.div(tt, xsize), lax.rem(tt, xsize))

    def mate(d):
        return lax.rem(t + d + T, T)

    def plane(d):
        return lax.rem(z + d + R, R)

    def remote(src, dst, ssem, rsem, target):
        return pltpu.make_async_remote_copy(
            src_ref=src, dst_ref=dst, send_sem=ssem, recv_sem=rsem,
            device_id=target, device_id_type=MESH,
        )

    weights = pltpu.make_async_copy(band.at[:, pl.ds(t * NCH, NCH)], wts, w_sem)
    local = []
    for c in range(NCH):
        col = pl.multiple_of(t * S + c * LANES, LANES)
        local.append(pltpu.make_async_copy(traces.at[:, pl.ds(col, LANES)], rx.at[c, 0], l_sem.at[c]))
    for copy in local:
        copy.start()
    weights.start()

    barrier = pltpu.get_barrier_semaphore()
    partners = [dev(z, mate(d)) for d in range(1, T)]
    partners += [dev(plane(d), t) for d in range(1, R)]
    partners += [dev(plane(dz), mate(dt)) for dz in (-1, 1) for dt in (-1, 1)]
    for p in partners:
        pl.semaphore_signal(barrier, inc=1, device_id=p, device_id_type=MESH)
    pl.semaphore_wait(barrier, len(partners))

    send_c, send_a = {}, {}
    for d in range(1, T):
        send_c[d] = remote(codes, crx.at[d], c_send.at[d], c_recv.at[d], dev(z, mate(d)))
        send_c[d].start()
    for c in range(NCH):
        for d in range(1, T):
            col = pl.multiple_of(mate(d) * S + c * LANES, LANES)
            send_a[c, d] = remote(
                traces.at[:, pl.ds(col, LANES)], rx.at[c, d],
                a_send.at[c * T + d], a_recv.at[c * T + d], dev(z, mate(d)),
            )
            send_a[c, d].start()

    def banded(pieces, lane_x, x):
        low, mid, high = pieces
        zero = jnp.zeros_like(mid)
        return jnp.where(
            lane_x == x - 1, low, jnp.where(lane_x == x, mid, jnp.where(lane_x == x + 1, high, zero))
        )

    q1 = 9 * CLASSES
    spread = (
        lax.div(lax.broadcasted_iota(jnp.int32, (q1, q1 * XL), 1), XL)
        == lax.broadcasted_iota(jnp.int32, (q1, q1 * XL), 0)
    ).astype(F32).astype(BF16)
    tiles = jnp.dot(k1[...], spread, preferred_element_type=F32)
    lane_x = lax.rem(lax.broadcasted_iota(jnp.int32, (ch, q1 * XL), 1), XL)
    pieces = [tiles[n * ch:(n + 1) * ch] for n in range(3)]
    for x in range(XL):
        t1[x * ch:(x + 1) * ch, :] = banded(pieces, lane_x, x).astype(BF16)

    spread = (
        lax.rem(lax.broadcasted_iota(jnp.int32, (ch, HR), 1), ch)
        == lax.broadcasted_iota(jnp.int32, (ch, HR), 0)
    ).astype(F32).astype(BF16)
    lane_x = lax.div(lax.broadcasted_iota(jnp.int32, (ch, HR), 1), ch)
    for q in range(9):
        tiles = jnp.dot(k2[q], spread, preferred_element_type=F32)
        pieces = [tiles[n * ch:(n + 1) * ch] for n in range(3)]
        for x in range(XL):
            t2[x * ch:(x + 1) * ch, q * HR:(q + 1) * HR] = banded(pieces, lane_x, x).astype(BF16)

    @pl.when(z == 0)
    def _():
        for ref in (vol, nxt, prv):
            ref[0:2] = jnp.zeros((2,) + ref.shape[1:], BF16)

    @pl.when(z == R - 1)
    def _():
        for ref in (vol, nxt, prv):
            ref[I + 2:I + 4] = jnp.zeros((2,) + ref.shape[1:], BF16)

    @pl.when(t == 0)
    def _():
        prv[...] = jnp.zeros(prv.shape, BF16)

    @pl.when(t == T - 1)
    def _():
        nxt[...] = jnp.zeros(nxt.shape, BF16)
        anx[...] = jnp.zeros(anx.shape, BF16)

    send_z, send_n = {}, {}
    for c in range(NCH):
        local[c].wait()
        for d in range(1, T):
            if c == 0:
                send_c[d].wait_recv()
            send_a[c, d].wait_recv()
        data = rx[c].reshape(T * rows, LANES)
        for d in list(range(1, R)) + [0]:
            slot = d if NCH > 1 else 0
            if c == 0:
                base = plane(d) * CELLS
                cell = lax.broadcasted_iota(jnp.int32, (CELLS, rows), 0) + base
                for s in range(T):
                    row = codes[0:1, :] if s == 0 else crx[s, 0:1, :]
                    oh[slot, :, s * rows:(s + 1) * rows] = jnp.where(cell == row, 1.0, 0.0).astype(BF16)
            total = jnp.dot(oh[slot], data, preferred_element_type=F32)
            if d == 0:
                own[c] = total
            else:
                txz[c, d] = total.astype(BF16)
                send_z[c, d] = remote(
                    txz.at[c, d], rz.at[c, d], z_send.at[c * R + d], z_recv.at[c * R + d], dev(plane(d), t)
                )
                send_z[c, d].start()
            if c == 0:
                count = lax.dot_general(
                    jnp.ones((8, T * rows), BF16), oh[slot], (((1,), (1,)), ((), ())),
                    preferred_element_type=F32,
                )
                if d == 0:
                    cown[...] = count
                else:
                    ctx[d] = count
                    send_n[d] = remote(ctx.at[d], crz.at[d], n_send.at[d], n_recv.at[d], dev(plane(d), t))
                    send_n[d].start()

    count = cown[...]
    for d in range(1, R):
        send_n[d].wait_recv()
        count = count + crz[d]
    fold = jnp.transpose(jnp.broadcast_to(jnp.maximum(count[0:1], 1.0), (LANES, CELLS)))
    to_before = remote(avg.at[0], anx, e_send, e_recv, dev(z, mate(-1)))
    for c in range(NCH):
        total = own[c]
        for d in range(1, R):
            send_z[c, d].wait_recv()
            total = total + rz[c, d].astype(F32)
        avg[c] = (total / fold).astype(BF16)
        if c == 0:
            @pl.when(t > 0)
            def _():
                to_before.start()

    weights.wait()
    for k in range(NCH - 1):
        moveout(avg[k], avg[k + 1], wts, vol, k, I, XL)

    @pl.when(t < T - 1)
    def _():
        to_before.wait_recv()

    moveout(avg[NCH - 1], anx[...], wts, vol, NCH - 1, I, XL)

    def border(dz, dt):
        here, there = {0: ((2, I), (2, I)), 1: ((I, 2), (0, 2)), -1: ((2, 2), (I + 2, 2))}[dz]
        src = vol.at[pl.ds(*here)]
        if dt == 0:
            dst = vol.at[pl.ds(*there)]
        elif dt == -1:
            src = src.at[:, :, pl.ds(0, LANES)]
            dst = nxt.at[pl.ds(*there)]
        else:
            src = src.at[:, :, pl.ds(S - LANES, LANES)]
            dst = prv.at[pl.ds(*there)]
        index = (dz + 1) * 3 + dt + 1
        return remote(src, dst, g_send.at[index], g_recv.at[index], dev(plane(dz), mate(dt)))

    def inside(dz, dt):
        return (z + dz >= 0) & (z + dz < R) & (t + dt >= 0) & (t + dt < T)

    ways = [(dz, dt) for dz in (-1, 1, 0) for dt in (-1, 0, 1) if (dz, dt) != (0, 0)]
    for dz, dt in ways:
        @pl.when(inside(dz, dt))
        def _(dz=dz, dt=dt):
            border(dz, dt).start()
    for dz, dt in ways:
        @pl.when(inside(-dz, -dt))
        def _(dz=dz, dt=dt):
            border(dz, dt).wait_recv()

    width = S + LANES
    half = lax.broadcasted_iota(jnp.int32, (VR, LANES), 1) < LANES // 2
    for r in range(I + 4):
        edge = jnp.where(half, nxt[r].astype(F32), prv[r].astype(F32))
        full = jnp.concatenate([vol[r].astype(F32), edge], axis=1)
        v3[r, 0:VR] = pltpu.roll(full, 1, 1).astype(BF16)
        v3[r, VR:2 * VR] = full.astype(BF16)
        v3[r, 2 * VR:3 * VR] = pltpu.roll(full, width - 1, 1).astype(BF16)
    lane = lax.broadcasted_iota(jnp.int32, (HR, width), 1)
    keep = (lane < S) | ((lane < S + LANES // 2) & (t < T - 1)) | ((lane >= S + LANES // 2) & (t > 0))
    for r in range(I + 2):
        total = jnp.dot(t1[...], v3[r:r + 3].reshape(9 * VR, width), preferred_element_type=F32)
        used = keep
        if r == 0:
            used = keep & (z > 0)
        if r == I + 1:
            used = keep & (z < R - 1)
        value = jnp.where(used, gelu(total), 0.0)
        h3[r, 0:HR] = pltpu.roll(value, 1, 1)[:, :S].astype(BF16)
        h3[r, HR:2 * HR] = value[:, :S].astype(BF16)
        h3[r, 2 * HR:3 * HR] = pltpu.roll(value, width - 1, 1)[:, :S].astype(BF16)

    for r in range(I):
        total = jnp.dot(t2[...], h3[r:r + 3].reshape(9 * HR, S), preferred_element_type=F32)
        outb[r] = total.astype(BF16).reshape(XL, ch, S)

    def tile(d):
        tt = mate(d)
        return outb.at[pl.ds(lax.div(tt, xsize) * BI, BI), pl.ds(lax.rem(tt, xsize) * BX, BX)]

    spot = out.at[:, :, :, pl.ds(pl.multiple_of(t * S, LANES), S)]
    send_y = {}
    for d in range(1, T):
        send_y[d] = remote(tile(d), spot, y_send.at[d], y_recv.at[d], dev(z, mate(d)))
        send_y[d].start()
    keep_own = pltpu.make_async_copy(tile(0), spot, o_sem)
    keep_own.start()
    keep_own.wait()
    for d in range(1, T):
        came = mate(-d)
        arrived = out.at[:, :, :, pl.ds(pl.multiple_of(came * S, LANES), S)]
        remote(tile(d), arrived, y_send.at[d], y_recv.at[d], dev(z, mate(d))).wait_recv()

    for copy in (send_c, send_a, send_z, send_n, send_y):
        for item in copy.values():
            item.wait_send()

    @pl.when(t > 0)
    def _():
        to_before.wait_send()

    for dz, dt in ways:
        @pl.when(inside(dz, dt))
        def _(dz=dz, dt=dt):
            border(dz, dt).wait_send()


def moveout(block, following, wts, vol, k, I, XL):
    bins = I * XL
    moved = []
    for c in range(CLASSES):
        both = jnp.concatenate(
            [block[c * bins:(c + 1) * bins], following[c * bins:(c + 1) * bins]], axis=1
        )
        moved.append(jnp.dot(both, wts[c, k], preferred_element_type=F32))
    for i in range(I):
        rows = jnp.concatenate([m[i * XL:(i + 1) * XL] for m in moved], axis=0)
        vol[2 + i, :, k * LANES:(k + 1) * LANES] = rows.astype(BF16)


def per_device(traces, trace_dest, trace_bin, trace_class, band_weights, conv_first, conv_second):
    inline_size = lax.axis_size("inline")
    xsize = lax.axis_size("xline")
    planes = inline_size // GI
    rows, samples = traces.shape
    ch = conv_first.shape[0]
    T = GI * xsize
    R = planes
    S = samples // T
    NCH = S // LANES
    I = GI * BI
    XL = xsize * BX
    CELLS = CLASSES * I * XL
    VR = CLASSES * XL
    HR = ch * XL
    nb, bw = band_weights.shape[1], band_weights.shape[-1]

    target = trace_dest.reshape(rows)
    dest_i, dest_x = target // xsize, target % xsize
    inner = (dest_i % GI) * BI + trace_bin // BX
    across = dest_x * BX + trace_bin % BX
    code = (dest_i // GI) * CELLS + (trace_class * I + inner) * XL + across
    codes = jnp.broadcast_to(code[None, :], (8, rows))
    band = band_weights.reshape(CLASSES, nb, 2 * bw, bw)
    k1 = jnp.transpose(conv_first, (3, 0, 2, 4, 1)).reshape(3 * ch, 9 * CLASSES)
    k2 = jnp.transpose(conv_second, (2, 4, 3, 0, 1)).reshape(9, 3 * ch, ch)

    vmem = pl.BlockSpec(memory_space=pltpu.VMEM)
    anyspace = pl.BlockSpec(memory_space=pl.ANY)
    dma = pltpu.SemaphoreType.DMA
    out = pl.pallas_call(
        functools.partial(kernel, planes, xsize, rows, samples, ch),
        out_shape=jax.ShapeDtypeStruct((BI, BX, ch, samples), BF16),
        in_specs=[anyspace, vmem, anyspace, vmem, vmem],
        out_specs=vmem,
        scratch_shapes=[
            pltpu.VMEM((NCH, T, rows, LANES), BF16),
            pltpu.VMEM((T, 8, rows), jnp.int32),
            pltpu.VMEM((R if NCH > 1 else 1, CELLS, T * rows), BF16),
            pltpu.VMEM((NCH, CELLS, LANES), F32),
            pltpu.VMEM((8, CELLS), F32),
            pltpu.VMEM((NCH, R, CELLS, LANES), BF16),
            pltpu.VMEM((NCH, R, CELLS, LANES), BF16),
            pltpu.VMEM((R, 8, CELLS), F32),
            pltpu.VMEM((R, 8, CELLS), F32),
            pltpu.VMEM((NCH, CELLS, LANES), BF16),
            pltpu.VMEM((CELLS, LANES), BF16),
            pltpu.VMEM((CLASSES, NCH, 2 * bw, bw), BF16),
            pltpu.VMEM((I + 4, VR, S), BF16),
            pltpu.VMEM((I + 4, VR, LANES), BF16),
            pltpu.VMEM((I + 4, VR, LANES), BF16),
            pltpu.VMEM((I + 4, 3 * VR, S + LANES), BF16),
            pltpu.VMEM((I + 2, 3 * HR, S), BF16),
            pltpu.VMEM((HR, 9 * VR), BF16),
            pltpu.VMEM((HR, 9 * HR), BF16),
            pltpu.VMEM((I, XL, ch, S), BF16),
            dma, dma((NCH,)), dma,
            dma((NCH * T,)), dma((NCH * T,)),
            dma((T,)), dma((T,)),
            dma((NCH * R,)), dma((NCH * R,)),
            dma((R,)), dma((R,)),
            dma, dma,
            dma((9,)), dma((9,)),
            dma((T,)), dma((T,)),
        ],
        compiler_params=pltpu.CompilerParams(
            collective_id=0, has_side_effects=True, vmem_limit_bytes=50 * 1024 * 1024
        ),
        name="regularize",
    )(traces, codes, band, k1, k2)
    return jnp.transpose(out, (2, 0, 1, 3))


def solution(mesh):
    return jax.shard_map(
        per_device,
        mesh=mesh,
        in_specs=(
            P(("inline", "xline"), None),
            P(("inline", "xline"), None),
            P(("inline", "xline")),
            P(("inline", "xline")),
            P(),
            P(),
            P(),
        ),
        out_specs=P(None, "inline", "xline", None),
        check_vma=False,
    )
```

time: 145 us -> 50.3 us (0.35)
  the two profiles are of different devices: /device:TPU:1 before, /device:TPU:0 now
where the time goes in v1:
time: 50.3 us; the launch traced here: 49.7 us
  Pallas kernels  44.4 us (88%)
  local copies, waits for them, and re-layouts  4.57 us (9%)
  other arithmetic  0.73 us (1%)
    pallas_call x1, Pallas kernels, per_device(): pl.pallas_call(functools.partial(kernel, planes, xsize, rows, samples, ch...  44.4 us
    transpose x1, local copies, waits for them, and re-layouts, per_device(): return jnp.transpose(out, (2, 0, 1, 3))  1.34 us
    unnamed x2, local copies, waits for them, and re-layouts  1.22 us

profile of v1, /device:TPU:0, one launch (start us, length us, event | category | flops | bytes accessed | tf_op | source)
XLA Modules:
  0.0 49.7 jit_solution(9560225111295055740)
XLA Ops:
  0.0 0.7 %fusion.5 = s32[256]{0:T(256)S(1)} fusion(s32[256]{0:T(256)} %param.9, s32[256]{0:T(256)} %param.10, s32[256]{0:T(256)} %bitcast.13), kind=kLoop, calls=%fused_computation.20 | loop fusion | flops 17152 | bytes 4096 | tf_op jit(solution)/shard_map/add | solution.py:320
  0.7 0.8 %copy.11 = bf16[3,32,3,3,8]{1,0,4,3,2:T(4,128)(2,1)S(1)} copy(bf16[3,32,3,3,8]{1,4,3,0,2:T(8,128)(2,1)} %bitcast.12) | data formatting | bytes 27648 | tf_op jit(solution)/shard_map/transpose | solution.py:323
  1.6 0.1 reshape.15
  1.7 0.1 copy.13.k1
  1.8 1.0 %copy.12 = bf16[3,3,3,32,32]{4,3,2,1,0:T(8,128)(2,1)S(1)} copy(bf16[3,3,3,32,32]{4,3,1,2,0:T(8,128)(2,1)} %bitcast.11) | data formatting | bytes 110592 | tf_op jit(solution)/shard_map/transpose | solution.py:324
  2.8 0.0 copy-start
  2.8 1.2 %copy-done = bf16[256,2048]{1,0:T(8,128)(2,1)S(1)} copy-done((bf16[256,2048]{1,0:T(8,128)(2,1)S(1)}, bf16[256,2048]{1,0:T(8,128)(2,1)}, u32[]{:S(2)}) %copy-start) | copy-done | bytes 1048600
  4.0 44.4 %regularize.1 = bf16[2,2,32,2048]{3,2,1,0:T(8,128)(2,1)S(1)} custom-call(bf16[256,2048]{1,0:T(8,128)(2,1)S(1)} %copy-done, s32[8,256]{1,0:T(8,128)S(1)} %broadcast_in_dim.2.codes, bf16[8,16,256,128]{3,2,1,0:T(8,128)(2,1)} %bitcast.10, bf16[96,72]{1,0:T(8,128)(2,1)S(1)} %copy.13.k1, bf16[9,96,32]{2,1,0:T(8,128)(2,1)S(1)} %bitcast.9), custom_call_target="tpu_custom_call" | custom-call | tf_op jit(solution)/shard_map/regularize/pallas_call | solution.py:329
  48.4 1.3 %copy.14 = bf16[32,2,2,2048]{3,2,1,0:T(2,128)(2,1)} copy(bf16[32,2,2,2048]{3,0,2,1:T(8,128)(2,1)S(1)} %bitcast.8) | data formatting | bytes 1048576 | tf_op jit(solution)/shard_map/transpose | solution.py:369
  (1 shorter events, 0.0 us)
Async XLA Ops:
  2.8 1.2 %copy-start = (bf16[256,2048]{1,0:T(8,128)(2,1)S(1)}, bf16[256,2048]{1,0:T(8,128)(2,1)}, u32[]{:S(2)}) copy-start(bf16[256,2048]{1,0:T(8,128)(2,1)} %traces.1) | copy-start | bytes 3145732

commit v2 on v1

v2 whole, which is shorter than its diff:
```python
import functools

import jax
import jax.numpy as jnp
from jax import lax
from jax.experimental import pallas as pl
from jax.experimental.pallas import tpu as pltpu
from jax.sharding import PartitionSpec as P

CLASSES = 8
BI = 2
BX = 2
GI = 2
LANES = 128
MESH = pl.DeviceIdType.MESH
F32 = jnp.float32
BF16 = jnp.bfloat16


def gelu(x):
    return 0.5 * x * (1.0 + jnp.tanh(0.7978845608028654 * (x + 0.044715 * (x * x * x))))


def split(value, size):
    if size & (size - 1):
        return lax.div(value, size), lax.rem(value, size)
    return value >> (size.bit_length() - 1), value & (size - 1)


def band_matrices(ch, XL, k1, k2, t1, t2):
    HR = ch * XL

    def banded(pieces, lane_x, x):
        low, mid, high = pieces
        zero = jnp.zeros_like(mid)
        return jnp.where(
            lane_x == x - 1, low, jnp.where(lane_x == x, mid, jnp.where(lane_x == x + 1, high, zero))
        )

    taps = [(di, dt) for di in range(3) for dt in range(3)]
    q1 = 9 * CLASSES
    lanes = lax.broadcasted_iota(jnp.int32, (q1, q1 * XL), 1)
    spread = jnp.where(
        split(lanes, XL)[0] == lax.broadcasted_iota(jnp.int32, (q1, q1 * XL), 0), 1.0, 0.0
    ).astype(BF16)
    pieces = []
    for dx in range(3):
        rows = jnp.concatenate([k1[di * 9 + dx * 3 + dt].astype(F32) for di, dt in taps], axis=0)
        pieces.append(
            lax.dot_general(
                rows.astype(BF16), spread, (((0,), (0,)), ((), ())), preferred_element_type=F32
            )
        )
    lane_x = split(lax.broadcasted_iota(jnp.int32, (ch, q1 * XL), 1), XL)[1]
    for x in range(XL):
        t1[x * ch:(x + 1) * ch, :] = banded(pieces, lane_x, x).astype(BF16)

    lane_x, lane_c = split(lax.broadcasted_iota(jnp.int32, (ch, HR), 1), ch)
    spread = jnp.where(lane_c == lax.broadcasted_iota(jnp.int32, (ch, HR), 0), 1.0, 0.0).astype(BF16)
    for q, (di, dt) in enumerate(taps):
        pieces = [
            jnp.dot(k2[di * 9 + dx * 3 + dt], spread, preferred_element_type=F32) for dx in range(3)
        ]
        for x in range(XL):
            t2[x * ch:(x + 1) * ch, q * HR:(q + 1) * HR] = banded(pieces, lane_x, x).astype(BF16)


def kernel(
    planes, xsize, rows, samples, ch,
    traces, target, bins, classes, band, k1, k2, out,
    codes, rx, crx, oh, own, cown, txz, rz, rl, ctx, crz, avg, anx, wts, vol, nxt, prv, v3, h3, t1, t2, outb,
    w_sem, l_sem, o_sem, a_send, a_recv, c_send, c_recv, z_send, z_recv, l_recv, n_send, n_recv,
    e_send, e_recv, g_send, g_recv, y_send, y_recv,
):
    T = GI * xsize
    R = planes
    S = samples // T
    NCH = S // LANES
    I = GI * BI
    XL = xsize * BX
    CELLS = CLASSES * I * XL
    VR = CLASSES * XL
    HR = ch * XL
    inline = lax.axis_index("inline")
    xline = lax.axis_index("xline")
    z = lax.div(inline, GI)
    t = lax.rem(inline, GI) * xsize + xline

    def dev(zz, tt):
        return (zz * GI + lax.div(tt, xsize), lax.rem(tt, xsize))

    def mate(d):
        return lax.rem(t + d + T, T)

    def plane(d):
        return lax.rem(z + d + R, R)

    def remote(src, dst, ssem, rsem, target):
        return pltpu.make_async_remote_copy(
            src_ref=src, dst_ref=dst, send_sem=ssem, recv_sem=rsem,
            device_id=target, device_id_type=MESH,
        )

    weights = pltpu.make_async_copy(band.at[:, pl.ds(t * NCH, NCH)], wts, w_sem)
    local = []
    for c in range(NCH):
        col = pl.multiple_of(t * S + c * LANES, LANES)
        local.append(pltpu.make_async_copy(traces.at[:, pl.ds(col, LANES)], rx.at[c, 0], l_sem.at[c]))
    for copy in local:
        copy.start()
    weights.start()

    dest_i, dest_x = split(target[...], xsize)
    dest_z, dest_a = split(dest_i, GI)
    bin_i, bin_x = split(bins[...], BX)
    code = dest_z * CELLS + (classes[...] * I + dest_a * BI + bin_i) * XL + dest_x * BX + bin_x
    codes[...] = jnp.broadcast_to(code, (8, rows))

    barrier = pltpu.get_barrier_semaphore()
    partners = [dev(z, mate(d)) for d in range(1, T)]
    partners += [dev(plane(d), t) for d in range(1, R)]
    partners += [dev(plane(dz), mate(dt)) for dz in (-1, 1) for dt in (-1, 1)]
    for p in partners:
        pl.semaphore_signal(barrier, inc=1, device_id=p, device_id_type=MESH)
    pl.semaphore_wait(barrier, len(partners))

    send_c, send_a = {}, {}
    for d in range(1, T):
        send_c[d] = remote(codes, crx.at[d], c_send.at[d], c_recv.at[d], dev(z, mate(d)))
        send_c[d].start()
    for c in range(NCH):
        for d in range(1, T):
            col = pl.multiple_of(mate(d) * S + c * LANES, LANES)
            send_a[c, d] = remote(
                traces.at[:, pl.ds(col, LANES)], rx.at[c, d],
                a_send.at[c * T + d], a_recv.at[c * T + d], dev(z, mate(d)),
            )
            send_a[c, d].start()

    @pl.when(z == 0)
    def _():
        for ref in (vol, nxt, prv):
            ref[0:2] = jnp.zeros((2,) + ref.shape[1:], BF16)

    @pl.when(z == R - 1)
    def _():
        for ref in (vol, nxt, prv):
            ref[I + 2:I + 4] = jnp.zeros((2,) + ref.shape[1:], BF16)

    @pl.when(t == 0)
    def _():
        prv[...] = jnp.zeros(prv.shape, BF16)

    @pl.when(t == T - 1)
    def _():
        nxt[...] = jnp.zeros(nxt.shape, BF16)
        anx[...] = jnp.zeros(anx.shape, BF16)

    cell = lax.broadcasted_iota(jnp.int32, (CELLS, rows), 0)
    for d in range(T):
        if d > 0:
            send_c[d].wait_recv()
        row = codes[0:1, :] if d == 0 else crx[d, 0:1, :]
        for r in range(R):
            oh[r, :, d * rows:(d + 1) * rows] = jnp.where(cell == row - r * CELLS, 1.0, 0.0).astype(BF16)

    send_z, send_n = {}, {}
    outer = (z == 0) | (z == R - 1)

    def mirror(p):
        return jnp.where(z < 2, p, 3 - p)

    def hop(c, p, dst, rsem, r):
        return remote(txz.at[c, p], dst, z_send.at[c * R + p], rsem, dev(r, t))

    def hops(c):
        return {
            (0, True): hop(c, 0, rl.at[c], l_recv.at[c], mirror(1)),
            (0, False): hop(c, 0, rz.at[c, 0], z_recv.at[c * R], mirror(2)),
            (1, True): hop(c, 1, rz.at[c, 1], z_recv.at[c * R + 1], mirror(2)),
            (1, False): hop(c, 1, rz.at[c, 1], z_recv.at[c * R + 1], mirror(0)),
            (2, True): hop(c, 2, rz.at[c, 2], z_recv.at[c * R + 2], mirror(1)),
            (3, False): hop(c, 3, rz.at[c, 3], z_recv.at[c * R + 3], mirror(3)),
        }

    for c in range(NCH):
        local[c].wait()
        for d in range(1, T):
            send_a[c, d].wait_recv()
        data = rx[c].reshape(T * rows, LANES)
        if R == 4:
            ways = hops(c)
            for p in range(4):
                r = mirror(jnp.where(outer, (3, 2, 1, 0)[p], (2, 0, 1, 3)[p]))
                total = jnp.dot(oh[r], data, preferred_element_type=F32)
                if p < 2:
                    txz[c, p] = total.astype(BF16)

                @pl.when(outer)
                def _(p=p, total=total):
                    if p == 2:
                        txz[c, p] = total.astype(BF16)
                    if p == 3:
                        own[c] = total
                    else:
                        ways[p, True].start()

                @pl.when(jnp.logical_not(outer))
                def _(p=p, total=total):
                    if p == 2:
                        own[c] = total
                    if p == 3:
                        ways[0, True].wait_recv()
                        txz[c, p] = (total + rl[c].astype(F32)).astype(BF16)
                    if p != 2:
                        ways[p, False].start()
        else:
            for d in list(range(1, R)) + [0]:
                total = jnp.dot(oh[plane(d)], data, preferred_element_type=F32)
                if d == 0:
                    own[c] = total
                else:
                    txz[c, d] = total.astype(BF16)
                    send_z[c, d] = hop(c, d, rz.at[c, d], z_recv.at[c * R + d], plane(d))
                    send_z[c, d].start()
        if c == 0:
            for d in list(range(1, R)) + [0]:
                count = lax.dot_general(
                    jnp.ones((8, T * rows), BF16), oh[plane(d)], (((1,), (1,)), ((), ())),
                    preferred_element_type=F32,
                )
                if d == 0:
                    cown[...] = count
                else:
                    ctx[d] = count
                    send_n[d] = remote(ctx.at[d], crz.at[d], n_send.at[d], n_recv.at[d], dev(plane(d), t))
                    send_n[d].start()
            band_matrices(ch, XL, k1, k2, t1, t2)

    count = cown[...]
    for d in range(1, R):
        send_n[d].wait_recv()
        count = count + crz[d]
    fold = jnp.transpose(jnp.broadcast_to(jnp.maximum(count[0:1], 1.0), (LANES, CELLS)))
    to_before = remote(avg.at[0], anx, e_send, e_recv, dev(z, mate(-1)))
    for c in range(NCH):
        if R == 4:
            ways = hops(c)

            @pl.when(outer)
            def _():
                ways[1, False].wait_recv()
                ways[3, False].wait_recv()
                own[c] = own[c] + rz[c, 1].astype(F32) + rz[c, 3].astype(F32)

            @pl.when(jnp.logical_not(outer))
            def _():
                for p in range(3):
                    ways[p, p == 2].wait_recv()
                own[c] = own[c] + rz[c, 0].astype(F32) + rz[c, 1].astype(F32) + rz[c, 2].astype(F32)

            total = own[c]
        else:
            total = own[c]
            for d in range(1, R):
                send_z[c, d].wait_recv()
                total = total + rz[c, d].astype(F32)
        avg[c] = (total / fold).astype(BF16)
        if c == 0:
            @pl.when(t > 0)
            def _():
                to_before.start()

    weights.wait()
    for k in range(NCH - 1):
        moveout(avg[k], avg[k + 1], wts, vol, k, I, XL)

    @pl.when(t < T - 1)
    def _():
        to_before.wait_recv()

    moveout(avg[NCH - 1], anx[...], wts, vol, NCH - 1, I, XL)

    def border(dz, dt):
        here, there = {0: ((2, I), (2, I)), 1: ((I, 2), (0, 2)), -1: ((2, 2), (I + 2, 2))}[dz]
        src = vol.at[pl.ds(*here)]
        if dt == 0:
            dst = vol.at[pl.ds(*there)]
        elif dt == -1:
            src = src.at[:, :, pl.ds(0, LANES)]
            dst = nxt.at[pl.ds(*there)]
        else:
            src = src.at[:, :, pl.ds(S - LANES, LANES)]
            dst = prv.at[pl.ds(*there)]
        index = (dz + 1) * 3 + dt + 1
        return remote(src, dst, g_send.at[index], g_recv.at[index], dev(plane(dz), mate(dt)))

    def inside(dz, dt):
        return (z + dz >= 0) & (z + dz < R) & (t + dt >= 0) & (t + dt < T)

    sides = [(0, -1), (0, 1), (-1, 0), (1, 0), (-1, -1), (-1, 1), (1, -1), (1, 1)]
    for dz, dt in sides:
        @pl.when(inside(dz, dt))
        def _(dz=dz, dt=dt):
            border(dz, dt).start()

    def arrive(pairs):
        for dz, dt in pairs:
            @pl.when(inside(-dz, -dt))
            def _(dz=dz, dt=dt):
                border(dz, dt).wait_recv()

    width = S + LANES
    half = lax.broadcasted_iota(jnp.int32, (VR, LANES), 1) < LANES // 2
    lane = lax.broadcasted_iota(jnp.int32, (HR, width), 1)
    keep = (lane < S) | ((lane < S + LANES // 2) & (t < T - 1)) | ((lane >= S + LANES // 2) & (t > 0))

    def spread(r):
        edge = jnp.where(half, nxt[r].astype(F32), prv[r].astype(F32))
        full = jnp.concatenate([vol[r].astype(F32), edge], axis=1)
        v3[r, 0:VR] = pltpu.roll(full, 1, 1).astype(BF16)
        v3[r, VR:2 * VR] = full.astype(BF16)
        v3[r, 2 * VR:3 * VR] = pltpu.roll(full, width - 1, 1).astype(BF16)

    def first(r):
        total = jnp.dot(t1[...], v3[pl.ds(r, 3)].reshape(9 * VR, width), preferred_element_type=F32)
        real = ((r > 0) | (z > 0)) & ((r < I + 1) | (z < R - 1))
        value = jnp.where(keep & real, gelu(total), 0.0)
        h3[r, 0:HR] = pltpu.roll(value, 1, 1)[:, :S].astype(BF16)
        h3[r, HR:2 * HR] = value[:, :S].astype(BF16)
        h3[r, 2 * HR:3 * HR] = pltpu.roll(value, width - 1, 1)[:, :S].astype(BF16)

    arrive(sides[:2])
    for r in range(2, I + 2):
        spread(r)
    for r in range(2, I):
        first(r)
    arrive(sides[2:])
    for r in (0, 1, I + 2, I + 3):
        spread(r)

    mine = lax.div(t, xsize)

    def shared(phase, k):
        a = 1 - mine if phase == 0 else mine
        b = lax.rem(xline + k, xsize)
        source = outb.at[pl.ds(a * BI, BI), pl.ds(b * BX, BX)]
        spot = out.at[:, :, :, pl.ds(pl.multiple_of(t * S, LANES), S)]
        index = phase * xsize + k
        if index == xsize:
            return pltpu.make_async_copy(source, spot, o_sem)
        return remote(source, spot, y_send.at[index], y_recv.at[index], dev(z, a * xsize + b))

    def landed(phase, k):
        a = 1 - mine if phase == 0 else mine
        b = lax.rem(xline - k + xsize, xsize)
        spot = out.at[:, :, :, pl.ds(pl.multiple_of((a * xsize + b) * S, LANES), S)]
        index = phase * xsize + k
        source = outb.at[pl.ds(a * BI, BI), pl.ds(b * BX, BX)]
        return remote(source, spot, y_send.at[index], y_recv.at[index], dev(z, a * xsize + b))

    for phase in range(2):
        a = 1 - mine if phase == 0 else mine
        for n in range(2):
            first(a * I + n)
        for n in range(BI):
            r = a * BI + n
            total = jnp.dot(t2[...], h3[pl.ds(r, 3)].reshape(9 * HR, S), preferred_element_type=F32)
            outb[r] = total.astype(BF16).reshape(XL, ch, S)
        for k in range(xsize):
            shared(phase, k).start()
    shared(1, 0).wait()
    for phase in range(2):
        for k in range(xsize):
            if (phase, k) != (1, 0):
                landed(phase, k).wait_recv()
                shared(phase, k).wait_send()

    for copy in (send_c, send_a, send_z, send_n):
        for item in copy.values():
            item.wait_send()
    if R == 4:
        for c in range(NCH):
            ways = hops(c)
            for p in range(2):
                ways[p, False].wait_send()

            @pl.when(outer)
            def _():
                ways[2, True].wait_send()

            @pl.when(jnp.logical_not(outer))
            def _():
                ways[3, False].wait_send()

    @pl.when(t > 0)
    def _():
        to_before.wait_send()

    for dz, dt in sides:
        @pl.when(inside(dz, dt))
        def _(dz=dz, dt=dt):
            border(dz, dt).wait_send()


def moveout(block, following, wts, vol, k, I, XL):
    bins = I * XL
    moved = []
    for c in range(CLASSES):
        both = jnp.concatenate(
            [block[c * bins:(c + 1) * bins], following[c * bins:(c + 1) * bins]], axis=1
        )
        moved.append(jnp.dot(both, wts[c, k], preferred_element_type=F32))
    for i in range(I):
        rows = jnp.concatenate([m[i * XL:(i + 1) * XL] for m in moved], axis=0)
        vol[2 + i, :, k * LANES:(k + 1) * LANES] = rows.astype(BF16)


def per_device(traces, trace_dest, trace_bin, trace_class, band_weights, conv_first, conv_second):
    inline_size = lax.axis_size("inline")
    xsize = lax.axis_size("xline")
    planes = inline_size // GI
    rows, samples = traces.shape
    ch = conv_first.shape[0]
    T = GI * xsize
    R = planes
    S = samples // T
    NCH = S // LANES
    I = GI * BI
    XL = xsize * BX
    CELLS = CLASSES * I * XL
    VR = CLASSES * XL
    HR = ch * XL
    nb, bw = band_weights.shape[1], band_weights.shape[-1]

    band = band_weights.reshape(CLASSES, nb, 2 * bw, bw)
    k1 = jnp.transpose(conv_first, (2, 3, 4, 1, 0)).reshape(27, CLASSES, ch)
    k2 = jnp.transpose(conv_second, (2, 3, 4, 0, 1)).reshape(27, ch, ch)

    vmem = pl.BlockSpec(memory_space=pltpu.VMEM)
    hbm = pl.BlockSpec(memory_space=pltpu.HBM)
    dma = pltpu.SemaphoreType.DMA
    out = pl.pallas_call(
        functools.partial(kernel, planes, xsize, rows, samples, ch),
        out_shape=jax.ShapeDtypeStruct((BI, BX, ch, samples), BF16),
        in_specs=[hbm, vmem, vmem, vmem, hbm, vmem, vmem],
        out_specs=vmem,
        scratch_shapes=[
            pltpu.VMEM((8, rows), jnp.int32),
            pltpu.VMEM((NCH, T, rows, LANES), BF16),
            pltpu.VMEM((T, 8, rows), jnp.int32),
            pltpu.VMEM((R, CELLS, T * rows), BF16),
            pltpu.VMEM((NCH, CELLS, LANES), F32),
            pltpu.VMEM((8, CELLS), F32),
            pltpu.VMEM((NCH, R, CELLS, LANES), BF16),
            pltpu.VMEM((NCH, R, CELLS, LANES), BF16),
            pltpu.VMEM((NCH, CELLS, LANES), BF16),
            pltpu.VMEM((R, 8, CELLS), F32),
            pltpu.VMEM((R, 8, CELLS), F32),
            pltpu.VMEM((NCH, CELLS, LANES), BF16),
            pltpu.VMEM((CELLS, LANES), BF16),
            pltpu.VMEM((CLASSES, NCH, 2 * bw, bw), BF16),
            pltpu.VMEM((I + 4, VR, S), BF16),
            pltpu.VMEM((I + 4, VR, LANES), BF16),
            pltpu.VMEM((I + 4, VR, LANES), BF16),
            pltpu.VMEM((I + 4, 3 * VR, S + LANES), BF16),
            pltpu.VMEM((I + 2, 3 * HR, S), BF16),
            pltpu.VMEM((HR, 9 * VR), BF16),
            pltpu.VMEM((HR, 9 * HR), BF16),
            pltpu.VMEM((I, XL, ch, S), BF16),
            dma, dma((NCH,)), dma,
            dma((NCH * T,)), dma((NCH * T,)),
            dma((T,)), dma((T,)),
            dma((NCH * R,)), dma((NCH * R,)), dma((NCH,)),
            dma((R,)), dma((R,)),
            dma, dma,
            dma((9,)), dma((9,)),
            dma((T,)), dma((T,)),
        ],
        compiler_params=pltpu.CompilerParams(
            collective_id=0, has_side_effects=True, vmem_limit_bytes=60 * 1024 * 1024
        ),
        name="regularize",
    )(
        traces, trace_dest.reshape(1, rows), trace_bin.reshape(1, rows), trace_class.reshape(1, rows),
        band, k1, k2,
    )
    return jnp.transpose(out, (2, 0, 1, 3))


def solution(mesh):
    return jax.shard_map(
        per_device,
        mesh=mesh,
        in_specs=(
            P(("inline", "xline"), None),
            P(("inline", "xline"), None),
            P(("inline", "xline")),
            P(("inline", "xline")),
            P(),
            P(),
            P(),
        ),
        out_specs=P(None, "inline", "xline", None),
        check_vma=False,
    )
```

time: 50.3 us -> 48 us (0.954)
  local copies, waits for them, and re-layouts: 4.57 us -> 2.38 us
  Pallas kernels: 44.4 us -> 45.5 us
  other arithmetic: 0.73 us -> 0 us
    transpose x2 -> x0, local copies, waits for them, and re-layouts: 1.81 us -> none  [the longest x1 0.96 us: per_device(): k2 = jnp.transpose(conv_second, (2, 4, 3, 0, 1)).reshape(9, 3 * ch, ch)]
    unnamed x2 -> x0, local copies, waits for them, and re-layouts: 1.22 us -> none
    pallas_call x1, Pallas kernels: 44.4 us -> 45.5 us  [per_device(): pl.pallas_call(functools.partial(kernel, planes, xsize, rows, samples, ch...]
    transpose x1, local copies, waits for them, and re-layouts: 1.34 us -> 2.38 us  [per_device(): return jnp.transpose(out, (2, 0, 1, 3))]
    add x1 -> x0, other arithmetic: 0.73 us -> none  [per_device(): code = dest_i // GI * CELLS + (trace_class * I + inner) * XL + across]
where the time goes in v2:
time: 48 us; the launch traced here: 47.9 us
  Pallas kernels  45.5 us (95%)
  local copies, waits for them, and re-layouts  2.38 us (5%)
    pallas_call x1, Pallas kernels, per_device(): pl.pallas_call(functools.partial(kernel, planes, xsize, rows, samples, ch...  45.5 us
    transpose x1, local copies, waits for them, and re-layouts, per_device(): return jnp.transpose(out, (2, 0, 1, 3))  2.38 us

profile of v2, /device:TPU:0, one launch (start us, length us, event | category | flops | bytes accessed | tf_op | source)
XLA Modules:
  0.0 47.9 jit_solution(8108389029225129664)
XLA Ops:
  0.0 45.5 %regularize.1 = bf16[2,2,32,2048]{3,2,1,0:T(8,128)(2,1)} custom-call(bf16[256,2048]{1,0:T(8,128)(2,1)} %traces.1, s32[1,256]{1,0:T(1,128)} %bitcast.15, s32[1,256]{1,0:T(1,128)} %bitcast.16, s32[1,256]{1,0:T(1,128)} %bitcast.17, bf16[8,16,256,128]{3,2,1,0:T(8,128)(2,1)} %bitcast.11, bf16[27,8,32]{2,1,0:T(8,128)(2,1)} %bitcast.14, bf16[27,32,32]{2,1,0:T(8,128)(2,1)} %bitcast.13), custom_call_target="tpu_custom_call" | custom-call | tf_op jit(solution)/shard_map/regularize/pallas_call | solution.py:443
  45.5 2.4 %copy.8 = bf16[32,2,2,2048]{3,2,1,0:T(2,128)(2,1)} copy(bf16[32,2,2,2048]{3,0,2,1:T(8,128)(2,1)} %bitcast.12) | data formatting | bytes 1048576 | tf_op jit(solution)/shard_map/transpose | solution.py:488
